TPU v7x, 256 devices: a whole 4x4x8 slice. The times are simulated.
256 devices in a mesh: row: 16 (over z_hi, y), col: 16 (over x, z_lo, core).
Axes of the slice: x: 4, y: 4, z: 8 (z_hi: 4, z_lo: 2; z = z_hi * 2 + z_lo), core: 2. Of those that a mesh axis runs over, the one named last changes fastest.
Arguments:
- opening_old: float32 [2048, 2048], P('row', 'col'), may hold values from 0.5 to 1.5
- pressure_old: float32 [2048, 2048], P('row', 'col'), may hold values from -4 to 4
- injection: float32 [2048, 2048], P('row', 'col'), may hold values from 0 to 2
- front_flags: int32 [16, 1024], P('row', 'col'), may hold values 0 or 1
- self_kernel: float32 [256, 256], replicated, may hold values from -0.375 to 0.375
- source_column: int32 [16, 1024, 4], P('row', 'col'), may hold values from 0 to 15, all different within a row; in each aligned block of 64 rows (0 to 63, 64 to 127, ..., all dimensions but the last counted through in order) at most 32 rows name the same one
- source_tile: int32 [16, 1024, 4], P('row', 'col'), may hold values from 0 to 63
- source_rank: int32 [16, 1024, 4], P('row', 'col'), may hold values from 1 to 16
- left_factor: float32 [16, 1024, 4, 16, 256], P('row', 'col'), may hold values from -1.5 to 1.5
- right_factor: float32 [16, 1024, 4, 16, 256], P('row', 'col'), may hold values from -0.375 to 0.375
Outputs:
- opening_new: float32 [2048, 2048], P('row', 'col')
- pressure_new: float32 [2048, 2048], P('row', 'col')
Inputs may be any that keep to these rules, and one draw needn't show every extreme that they name: `source_column`: the 4 sources of a target tile lie in 4 different column blocks; among the 64 target tiles of one device no column block is named more than 32 times, and that count is reached.
All inputs are finite; a program needn't handle non-finite values. No bound on the sum of `front_flags` on one device may be relied on, other than what follows from the above.
Results may differ from a plain program's by a relative error of at most 0.000076.
Values sent between devices are 32-bit elements; how exact they have to be, the bound alone decides.
A program may use at most 64 MiB of HBM per device.

v0:
```python
import jax
import jax.numpy as jnp
from jax import lax
from jax.sharding import PartitionSpec as P

TSIDE = 16
PASSES = 3


step_size = 0.1
highest_mode = lax.Precision.HIGHEST


def with_halo(array, sides, width):
    for axis, dim in sides:
        devices, length = (lax.axis_size(axis), array.shape[dim])
        up = [(i, (i + 1) % devices) for i in range(devices - 1)]
        down = [(j, i) for i, j in up]
        last = lax.slice_in_dim(array, length - width, length, axis=dim)
        leading = lax.slice_in_dim(array, 0, width, axis=dim)
        before = lax.ppermute(last, axis, up)
        after = lax.ppermute(leading, axis, down)
        array = jnp.concatenate([before, array, after], axis=dim)
    return array


def picard_pass(wide_open, wide_press, start_open, inject_part):
    row_count = wide_open.shape[0] - 2
    col_count = wide_open.shape[1] - 2
    cubed_open = wide_open * wide_open * wide_open

    def offset(array, shift_row, shift_col):
        return array[
            1 + shift_row : 1 + shift_row + row_count, 1 + shift_col : 1 + shift_col + col_count
        ]

    cube_middle = offset(cubed_open, 0, 0)
    press_middle = offset(wide_press, 0, 0)
    accumulated = jnp.zeros_like(cube_middle)
    for shift_row, shift_col in ((1, 0), (-1, 0), (0, 1), (0, -1)):
        conduct = (cube_middle + offset(cubed_open, shift_row, shift_col)) / 24.0
        accumulated = accumulated + conduct * (
            offset(wide_press, shift_row, shift_col) - press_middle
        )
    return start_open + step_size * (accumulated + inject_part)


def to_tiles(field_block):
    row_tiles = field_block.shape[0] // TSIDE
    col_tiles = field_block.shape[1] // TSIDE
    shaped = field_block.reshape(row_tiles, TSIDE, col_tiles, TSIDE).transpose(0, 2, 1, 3)
    return shaped.reshape(row_tiles * col_tiles, TSIDE * TSIDE)


def from_tiles(tile_rows, row_tiles, col_tiles):
    shaped = tile_rows.reshape(row_tiles, col_tiles, TSIDE, TSIDE).transpose(0, 2, 1, 3)
    return shaped.reshape(row_tiles * TSIDE, col_tiles * TSIDE)


def local(
    opening_old,
    pressure_old,
    injection,
    front_flags,
    self_kernel,
    source_column,
    source_tile,
    source_rank,
    left_factor,
    right_factor,
):
    block_rows, block_cols = opening_old.shape
    first = with_halo(jnp.stack([opening_old, pressure_old]), (("row", 1), ("col", 2)), 1)
    wide_press = first[1]
    current = picard_pass(first[0], wide_press, opening_old, injection)
    for passes_done in range(1, PASSES):
        wide_open = with_halo(current, (("row", 0), ("col", 1)), 1)
        current = picard_pass(wide_open, wide_press, opening_old, injection)
    row_tiles = block_rows // TSIDE
    col_tiles = block_cols // TSIDE
    tile_rows = to_tiles(current) * front_flags[0][:, None].astype(jnp.float32)
    opening_new = from_tiles(tile_rows, row_tiles, col_tiles)
    tile_count = tile_rows.shape[0]
    links = source_column.shape[2]
    columns = source_column[0].reshape(-1)
    picks = source_tile[0].reshape(-1)
    band = lax.all_gather(tile_rows, "col", axis=0, tiled=True)
    sources = band[columns * tile_count + picks]
    sources = sources.reshape(tile_count, links, -1)
    rank_keep = (
        jnp.arange(right_factor.shape[3], dtype=jnp.int32)[None, None, :]
        < source_rank[0][:, :, None]
    ).astype(jnp.float32)
    coefficients = (
        jnp.einsum("tkjs,tks->tkj", right_factor[0], sources, precision=highest_mode) * rank_keep
    )
    near_terms = jnp.einsum("tkjs,tkj->ts", left_factor[0], coefficients, precision=highest_mode)
    self_terms = jnp.einsum("su,tu->ts", self_kernel, tile_rows, precision=highest_mode)
    pressure_new = from_tiles(self_terms + near_terms, row_tiles, col_tiles)
    return (opening_new, pressure_new)


def solution(mesh):
    return jax.shard_map(
        local,
        mesh=mesh,
        in_specs=(
            P("row", "col"),
            P("row", "col"),
            P("row", "col"),
            P("row", "col"),
            P(),
            P("row", "col", None),
            P("row", "col", None),
            P("row", "col", None),
            P("row", "col", None, None, None),
            P("row", "col", None, None, None),
        ),
        out_specs=(P("row", "col"), P("row", "col")),
        check_vma=False,
    )
```

profile of v0, /device:TPU:1, one launch (start us, length us, event | category | flops | bytes accessed | tf_op | source)
XLA Modules:
  0.0 133.9 jit_solution(10966128705149386193)
XLA Ops:
  7.3 0.8 pad_maximum_fusion.5
  8.0 1.3 collective-permute-start.1
  9.3 4.7 %collective-permute-start = (f32[2,1,128]{2,1,0:T(1,128)S(1)}, f32[2,1,128]{2,1,0:T(1,128)S(1)}, u32[]{:S(2)}, u32[]{:S(2)}) collective-permute-start(f32[2,1,128]{2,1,0:T(1,128)S(1)} %get-tuple-element.6), channel_id=1, source_target_pairs={{0,16},{16,32},{32,48},{48,64},{64,80},{80,96},{96,112},{112,128},... | collective-permute-start | bytes 3080 | tf_op jit(solution)/shard_map/ppermute | solution.py:21
  14.0 0.7 collective-permute-done
  14.7 0.9 pad_maximum_fusion.1
  15.7 5.6 %collective-permute-start.3 = (f32[2,130,1]{2,1,0:T(8,128)S(1)}, f32[2,130,1]{2,1,0:T(8,128)S(1)}, u32[]{:S(2)}, u32[]{:S(2)}) collective-permute-start(f32[2,130,1]{2,1,0:T(8,128)S(1)} %get-tuple-element.5), channel_id=1, source_target_pairs={{1,0},{2,1},{3,2},{4,3},{5,4},{6,5},{7,6},{8,7},{9,8},{10,9},{11,1... | collective-permute-start | bytes 3128 | tf_op jit(solution)/shard_map/ppermute | solution.py:22
  21.3 1.9 %collective-permute-start.2 = (f32[2,130,1]{2,1,0:T(8,128)S(1)}, f32[2,130,1]{2,1,0:T(8,128)S(1)}, u32[]{:S(2)}, u32[]{:S(2)}) collective-permute-start(f32[2,130,1]{2,1,0:T(8,128)S(1)} %get-tuple-element.4), channel_id=1, source_target_pairs={{0,1},{1,2},{2,3},{3,4},{4,5},{5,6},{6,7},{7,8},{8,9},{9,10},{10,1... | collective-permute-start | bytes 3128 | tf_op jit(solution)/shard_map/ppermute | solution.py:21
  23.2 0.6 collective-permute-done.3
  23.8 1.4 %collective-permute-done.2 = f32[2,130,1]{2,1,0:T(8,128)S(1)} collective-permute-done((f32[2,130,1]{2,1,0:T(8,128)S(1)}, f32[2,130,1]{2,1,0:T(8,128)S(1)}, u32[]{:S(2)}, u32[]{:S(2)}) %collective-permute-start.2) | collective-permute-done | bytes 1072 | tf_op jit(solution)/shard_map/ppermute | solution.py:21
  25.2 1.1 pad_maximum_fusion
  26.4 1.1 fusion.38
  27.5 1.3 collective-permute-start.5
  28.8 4.5 %collective-permute-start.4 = (f32[1,128]{1,0:T(1,128)S(1)}, f32[1,128]{1,0:T(1,128)S(1)}, u32[]{:S(2)}, u32[]{:S(2)}) collective-permute-start(f32[1,128]{1,0:T(1,128)S(1)} %get-tuple-element.14), channel_id=1, source_target_pairs={{0,16},{16,32},{32,48},{48,64},{64,80},{80,96},{96,112},{112,128},... | collective-permute-start | bytes 1544 | tf_op jit(solution)/shard_map/ppermute | solution.py:21
  33.3 0.7 collective-permute-done.4
  34.1 2.2 %collective-permute-start.7 = (f32[130,1]{1,0:T(8,128)S(1)}, f32[130,1]{1,0:T(8,128)S(1)}, u32[]{:S(2)}, u32[]{:S(2)}) collective-permute-start(f32[130,1]{1,0:T(8,128)S(1)} %get-tuple-element.11), channel_id=1, source_target_pairs={{1,0},{2,1},{3,2},{4,3},{5,4},{6,5},{7,6},{8,7},{9,8},{10,9},{11,1... | collective-permute-start | bytes 1568 | tf_op jit(solution)/shard_map/ppermute | solution.py:22
  36.3 4.9 %collective-permute-start.6 = (f32[130,1]{1,0:T(8,128)S(1)}, f32[130,1]{1,0:T(8,128)S(1)}, u32[]{:S(2)}, u32[]{:S(2)}) collective-permute-start(f32[130,1]{1,0:T(8,128)S(1)} %get-tuple-element.10), channel_id=1, source_target_pairs={{0,1},{1,2},{2,3},{3,4},{4,5},{5,6},{6,7},{7,8},{8,9},{9,10},{10,1... | collective-permute-start | bytes 1568 | tf_op jit(solution)/shard_map/ppermute | solution.py:21
  41.3 1.3 collective-permute-done.6
  42.7 1.1 fusion.24
  43.8 1.3 collective-permute-start.9
  45.1 4.5 %collective-permute-start.8 = (f32[1,128]{1,0:T(1,128)S(1)}, f32[1,128]{1,0:T(1,128)S(1)}, u32[]{:S(2)}, u32[]{:S(2)}) collective-permute-start(f32[1,128]{1,0:T(1,128)S(1)} %get-tuple-element.12), channel_id=1, source_target_pairs={{0,16},{16,32},{32,48},{48,64},{64,80},{80,96},{96,112},{112,128},... | collective-permute-start | bytes 1544 | tf_op jit(solution)/shard_map/ppermute | solution.py:21
  49.7 0.7 collective-permute-done.8
  50.5 1.9 %collective-permute-start.11 = (f32[130,1]{1,0:T(8,128)S(1)}, f32[130,1]{1,0:T(8,128)S(1)}, u32[]{:S(2)}, u32[]{:S(2)}) collective-permute-start(f32[130,1]{1,0:T(8,128)S(1)} %get-tuple-element.9), channel_id=1, source_target_pairs={{1,0},{2,1},{3,2},{4,3},{5,4},{6,5},{7,6},{8,7},{9,8},{10,9},{11,1... | collective-permute-start | bytes 1568 | tf_op jit(solution)/shard_map/ppermute | solution.py:22
  52.4 5.1 %collective-permute-start.10 = (f32[130,1]{1,0:T(8,128)S(1)}, f32[130,1]{1,0:T(8,128)S(1)}, u32[]{:S(2)}, u32[]{:S(2)}) collective-permute-start(f32[130,1]{1,0:T(8,128)S(1)} %get-tuple-element.8), channel_id=1, source_target_pairs={{0,1},{1,2},{2,3},{3,4},{4,5},{5,6},{6,7},{7,8},{8,9},{9,10},{10,1... | collective-permute-start | bytes 1568 | tf_op jit(solution)/shard_map/ppermute | solution.py:21
  57.9 0.9 collective-permute-done.10
  59.0 0.8 fusion.47
  60.4 0.7 broadcast_multiply_fusion
  61.5 53.2 %all-gather.2.cloned.1.call-done = f32[1024,256]{1,0:T(8,128)} async-done(((f32[64,256]{1,0:T(8,128)}), f32[1024,256]{1,0:T(8,128)}) %all-gather.2.cloned.1.call-update) | async-done | bytes 1048592 | tf_op jit(solution)/shard_map/all_gather | solution.py:87
  114.7 2.2 %gather_fusion = f32[256,256]{1,0:T(8,128)S(1)} fusion(f32[1024,256]{1,0:T(8,128)} %all-gather.2.cloned.1.call-done, s32[1024]{0:T(1024)S(1)} %pad_clamp_fusion), kind=kCustom, calls=%fused_computation | custom fusion | bytes 525312 | tf_op jit(solution)/shard_map/gather | solution.py:88
  117.1 5.9 %fusion.2 = f32[64,4,1,16]{3,2,1,0:T(1,128)S(1)} fusion(f32[64,4,256,1]{2,3,1,0:T(1,128)S(1)} %reshape.88, f32[1,64,4,16,256]{4,3,2,1,0:T(8,128)} %param.19), kind=kOutput, calls=%fused_computation.3 | convolution fusion | flops 12582912 | bytes 4472832 | tf_op jit(solution)/shard_map/tkjs,tks->tkj/dot_general | solution.py:95
  123.2 2.4 %fusion = f32[64,1,256,1]{2,1,3,0:T(1,128)S(1)} fusion(f32[64,4,16,1]{2,3,1,0:T(1,128)S(1)} %bitcast.48, f32[1,64,4,16,256]{4,3,2,1,0:T(8,128)S(1)} %copy-done.1), kind=kOutput, calls=%fused_computation.1 | convolution fusion | flops 12582912 | bytes 4276224 | tf_op jit(solution)/shard_map/tkjs,tkj->ts/dot_general | solution.py:97
  125.5 0.4 convolution_add_fusion
  126.3 0.8 reshape.74
  (54 shorter events, 2.7 us)
Async XLA Ops:
  7.2 118.4 %copy-start = (f32[256,256]{1,0:T(8,128)S(1)}, f32[256,256]{1,0:T(8,128)}, u32[]{:S(2)}) copy-start(f32[256,256]{1,0:T(8,128)} %param.14) | copy-start | bytes 786436
  7.2 51.8 %copy-start.2 = (f32[128,128]{1,0:T(8,128)S(1)}, f32[128,128]{1,0:T(8,128)}, u32[]{:S(2)}) copy-start(f32[128,128]{1,0:T(8,128)} %param.10) | copy-start | bytes 196612
  7.2 51.8 %copy-start.4 = (f32[128,128]{1,0:T(8,128)S(1)}, f32[128,128]{1,0:T(8,128)}, u32[]{:S(2)}) copy-start(f32[128,128]{1,0:T(8,128)} %param.12) | copy-start | bytes 196612
  7.2 42.5 %copy-start.8 = (s32[1,64]{1,0:T(1,128)S(1)}, s32[1,64]{1,0:T(1,128)}, u32[]{:S(2)}) copy-start(s32[1,64]{1,0:T(1,128)} %param.13) | copy-start | bytes 772
  7.2 107.4 %all-gather.2.cloned.1.call-start = ((), (), s32[]{:S(2)}) async-start(), calls=%async_computation | async-start | bytes 1114112 | tf_op jit(solution)/shard_map/all_gather | solution.py:87
  8.0 6.0 %collective-permute-start.1 = (f32[2,1,128]{2,1,0:T(1,128)S(1)}, f32[2,1,128]{2,1,0:T(1,128)S(1)}, u32[]{:S(2)}, u32[]{:S(2)}) collective-permute-start(f32[2,1,128]{2,1,0:T(1,128)S(1)} %get-tuple-element.7), channel_id=1, source_target_pairs={{16,0},{32,16},{48,32},{64,48},{80,64},{96,80},{112,96},{128,112},... | collective-permute-start | bytes 3080 | tf_op jit(solution)/shard_map/ppermute | solution.py:22
  9.3 5.4 %collective-permute-start = (f32[2,1,128]{2,1,0:T(1,128)S(1)}, f32[2,1,128]{2,1,0:T(1,128)S(1)}, u32[]{:S(2)}, u32[]{:S(2)}) collective-permute-start(f32[2,1,128]{2,1,0:T(1,128)S(1)} %get-tuple-element.6), channel_id=1, source_target_pairs={{0,16},{16,32},{32,48},{48,64},{64,80},{80,96},{96,112},{112,128},... | collective-permute-start | bytes 3080 | tf_op jit(solution)/shard_map/ppermute | solution.py:21
  15.7 8.1 %collective-permute-start.3 = (f32[2,130,1]{2,1,0:T(8,128)S(1)}, f32[2,130,1]{2,1,0:T(8,128)S(1)}, u32[]{:S(2)}, u32[]{:S(2)}) collective-permute-start(f32[2,130,1]{2,1,0:T(8,128)S(1)} %get-tuple-element.5), channel_id=1, source_target_pairs={{1,0},{2,1},{3,2},{4,3},{5,4},{6,5},{7,6},{8,7},{9,8},{10,9},{11,1... | collective-permute-start | bytes 3128 | tf_op jit(solution)/shard_map/ppermute | solution.py:22
  21.3 3.9 %collective-permute-start.2 = (f32[2,130,1]{2,1,0:T(8,128)S(1)}, f32[2,130,1]{2,1,0:T(8,128)S(1)}, u32[]{:S(2)}, u32[]{:S(2)}) collective-permute-start(f32[2,130,1]{2,1,0:T(8,128)S(1)} %get-tuple-element.4), channel_id=1, source_target_pairs={{0,1},{1,2},{2,3},{3,4},{4,5},{5,6},{6,7},{7,8},{8,9},{9,10},{10,1... | collective-permute-start | bytes 3128 | tf_op jit(solution)/shard_map/ppermute | solution.py:21
  26.3 34.8 %copy-start.5 = (s32[1,64,4]{1,2,0:T(4,128)S(1)}, s32[1,64,4]{1,2,0:T(4,128)}, u32[]{:S(2)}) copy-start(s32[1,64,4]{1,2,0:T(4,128)} %param.16) | copy-start | bytes 3076
  26.3 34.8 %copy-start.6 = (s32[1,64,4]{1,2,0:T(4,128)S(1)}, s32[1,64,4]{1,2,0:T(4,128)}, u32[]{:S(2)}) copy-start(s32[1,64,4]{1,2,0:T(4,128)} %param.15) | copy-start | bytes 3076
  26.3 35.0 %copy-start.7 = (s32[1,64,4]{1,2,0:T(4,128)S(1)}, s32[1,64,4]{1,2,0:T(4,128)}, u32[]{:S(2)}) copy-start(s32[1,64,4]{1,2,0:T(4,128)} %param.17) | copy-start | bytes 3076
  27.5 5.8 %collective-permute-start.5 = (f32[1,128]{1,0:T(1,128)S(1)}, f32[1,128]{1,0:T(1,128)S(1)}, u32[]{:S(2)}, u32[]{:S(2)}) collective-permute-start(f32[1,128]{1,0:T(1,128)S(1)} %get-tuple-element.15), channel_id=1, source_target_pairs={{16,0},{32,16},{48,32},{64,48},{80,64},{96,80},{112,96},{128,112},... | collective-permute-start | bytes 1544 | tf_op jit(solution)/shard_map/ppermute | solution.py:22
  28.8 5.2 %collective-permute-start.4 = (f32[1,128]{1,0:T(1,128)S(1)}, f32[1,128]{1,0:T(1,128)S(1)}, u32[]{:S(2)}, u32[]{:S(2)}) collective-permute-start(f32[1,128]{1,0:T(1,128)S(1)} %get-tuple-element.14), channel_id=1, source_target_pairs={{0,16},{16,32},{32,48},{48,64},{64,80},{80,96},{96,112},{112,128},... | collective-permute-start | bytes 1544 | tf_op jit(solution)/shard_map/ppermute | solution.py:21
  34.1 7.2 %collective-permute-start.7 = (f32[130,1]{1,0:T(8,128)S(1)}, f32[130,1]{1,0:T(8,128)S(1)}, u32[]{:S(2)}, u32[]{:S(2)}) collective-permute-start(f32[130,1]{1,0:T(8,128)S(1)} %get-tuple-element.11), channel_id=1, source_target_pairs={{1,0},{2,1},{3,2},{4,3},{5,4},{6,5},{7,6},{8,7},{9,8},{10,9},{11,1... | collective-permute-start | bytes 1568 | tf_op jit(solution)/shard_map/ppermute | solution.py:22
  36.3 6.3 %collective-permute-start.6 = (f32[130,1]{1,0:T(8,128)S(1)}, f32[130,1]{1,0:T(8,128)S(1)}, u32[]{:S(2)}, u32[]{:S(2)}) collective-permute-start(f32[130,1]{1,0:T(8,128)S(1)} %get-tuple-element.10), channel_id=1, source_target_pairs={{0,1},{1,2},{2,3},{3,4},{4,5},{5,6},{6,7},{7,8},{8,9},{9,10},{10,1... | collective-permute-start | bytes 1568 | tf_op jit(solution)/shard_map/ppermute | solution.py:21
  43.8 5.8 %collective-permute-start.9 = (f32[1,128]{1,0:T(1,128)S(1)}, f32[1,128]{1,0:T(1,128)S(1)}, u32[]{:S(2)}, u32[]{:S(2)}) collective-permute-start(f32[1,128]{1,0:T(1,128)S(1)} %get-tuple-element.13), channel_id=1, source_target_pairs={{16,0},{32,16},{48,32},{64,48},{80,64},{96,80},{112,96},{128,112},... | collective-permute-start | bytes 1544 | tf_op jit(solution)/shard_map/ppermute | solution.py:22
  45.1 5.2 %collective-permute-start.8 = (f32[1,128]{1,0:T(1,128)S(1)}, f32[1,128]{1,0:T(1,128)S(1)}, u32[]{:S(2)}, u32[]{:S(2)}) collective-permute-start(f32[1,128]{1,0:T(1,128)S(1)} %get-tuple-element.12), channel_id=1, source_target_pairs={{0,16},{16,32},{32,48},{48,64},{64,80},{80,96},{96,112},{112,128},... | collective-permute-start | bytes 1544 | tf_op jit(solution)/shard_map/ppermute | solution.py:21
  50.5 7.5 %collective-permute-start.11 = (f32[130,1]{1,0:T(8,128)S(1)}, f32[130,1]{1,0:T(8,128)S(1)}, u32[]{:S(2)}, u32[]{:S(2)}) collective-permute-start(f32[130,1]{1,0:T(8,128)S(1)} %get-tuple-element.9), channel_id=1, source_target_pairs={{1,0},{2,1},{3,2},{4,3},{5,4},{6,5},{7,6},{8,7},{9,8},{10,9},{11,1... | collective-permute-start | bytes 1568 | tf_op jit(solution)/shard_map/ppermute | solution.py:22
  52.4 6.5 %collective-permute-start.10 = (f32[130,1]{1,0:T(8,128)S(1)}, f32[130,1]{1,0:T(8,128)S(1)}, u32[]{:S(2)}, u32[]{:S(2)}) collective-permute-start(f32[130,1]{1,0:T(8,128)S(1)} %get-tuple-element.8), channel_id=1, source_target_pairs={{0,1},{1,2},{2,3},{3,4},{4,5},{5,6},{6,7},{7,8},{8,9},{9,10},{10,1... | collective-permute-start | bytes 1568 | tf_op jit(solution)/shard_map/ppermute | solution.py:21
  117.1 6.0 %copy-start.1 = (f32[1,64,4,16,256]{4,3,2,1,0:T(8,128)S(1)}, f32[1,64,4,16,256]{4,3,2,1,0:T(8,128)}, u32[]{:S(2)}) copy-start(f32[1,64,4,16,256]{4,3,2,1,0:T(8,128)} %param.18) | copy-start | bytes 12582916
  117.1 8.4 %copy-start.3 = (f32[64,256]{1,0:T(8,128)S(1)}, f32[64,256]{1,0:T(8,128)}, u32[]{:S(2)}) copy-start(f32[64,256]{1,0:T(8,128)} %broadcast_multiply_fusion) | copy-start | bytes 196612
Sparse Core Ops, SparseCore 0:
  61.2 53.3 all-gather.1
where the time goes:
time: 135 us; the launch traced here: 134 us
  waiting for transfers between devices  59.5 us (44%)
  starting transfers between devices  39.3 us (29%)
  between operations  14.5 us (11%)
  matrix products  8.59 us (6%)
  other arithmetic  6.9 us (5%)
  local copies, waits for them, and re-layouts  5.14 us (4%)
    all_gather x1, waiting for transfers between devices, local(): band = lax.all_gather(tile_rows, 'col', axis=0, tiled=True)  53.2 us
    ppermute x6, starting transfers between devices, with_halo(): before = lax.ppermute(last, axis, up)  25.6 us
    ppermute x6, starting transfers between devices, with_halo(): after = lax.ppermute(leading, axis, down)  13.6 us
    dot_general x1, matrix products, local(): jnp.einsum('tkjs,tks->tkj', right_factor[0], sources, precision=highest_m...  5.86 us
    ppermute x6, waiting for transfers between devices, with_halo(): before = lax.ppermute(last, axis, up)  5.71 us
  transfers between devices with their start and end apart: 13, of which 8 were waited for; matrix products, arithmetic and copies ran while one was open for 1% of the time, Pallas kernels for 0%

commit v1 on v0

v1 whole, which is shorter than its diff:
```python
import functools

import jax
import jax.numpy as jnp
from jax import lax
from jax.experimental import pallas as pl
from jax.experimental.pallas import tpu as pltpu
from jax.sharding import PartitionSpec as P

TSIDE = 16
PASSES = 3
STEP = 0.1
MESH = pl.DeviceIdType.MESH
F32 = jnp.float32
HIGHEST = lax.Precision.HIGHEST


def swap_blocks(parts):
    parts = list(parts)
    block = lax.broadcasted_iota(jnp.int32, (8, 128), 1) // TSIDE
    for bit in (1, 2, 4):
        upper = (block & bit) != 0
        for i in range(8):
            if i & bit:
                continue
            a, b = parts[i], parts[i + bit]
            parts[i] = jnp.where(upper, pltpu.roll(b, TSIDE * bit, 1), a)
            parts[i + bit] = jnp.where(upper, b, pltpu.roll(a, 128 - TSIDE * bit, 1))
    return parts


def split_bf16(x):
    high = x.astype(jnp.bfloat16)
    low = (x - high.astype(F32)).astype(jnp.bfloat16)
    return high, low


def kernel(
    rows, cols,
    opening_ref, pressure_ref, injection_ref, flags_ref, self_ref,
    column_ref, tile_ref, rank_ref, left_ref, right_ref,
    opening_out, pressure_out,
    field, turned, edge_rows, edge_cols, middle, band, left, right, self_kernel, flags, near,
    column, tile, rank,
    field_sem, small_sem, factor_sem, edge_send, edge_recv, band_send, band_recv,
):
    r, c = lax.axis_index("row"), lax.axis_index("col")
    north, south = lax.rem(r + rows - 1, rows), lax.rem(r + 1, rows)
    west, east = lax.rem(c + cols - 1, cols), lax.rem(c + 1, cols)
    neighbours = [(north, c), (south, c), (north, west), (north, east), (south, west), (south, east)]

    barrier = pltpu.get_barrier_semaphore()
    for target in neighbours:
        pl.semaphore_signal(barrier, inc=1, device_id=target, device_id_type=MESH)
    for step in range(1, cols):
        pl.semaphore_signal(
            barrier, inc=1, device_id=(r, lax.rem(c + step, cols)), device_id_type=MESH
        )

    field_copies = [
        pltpu.make_async_copy(ref, field.at[i], field_sem.at[i])
        for i, ref in enumerate((opening_ref, pressure_ref, injection_ref))
    ]
    small_copies = [
        pltpu.make_async_copy(ref, to, small_sem.at[i])
        for i, (ref, to) in enumerate(
            ((flags_ref, flags), (self_ref, self_kernel), (column_ref, column), (tile_ref, tile), (rank_ref, rank))
        )
    ]
    factor_copies = [
        pltpu.make_async_copy(right_ref, right, factor_sem.at[0]),
        pltpu.make_async_copy(left_ref, left, factor_sem.at[1]),
    ]
    for copy in field_copies + small_copies + factor_copies:
        copy.start()
    for copy in field_copies:
        copy.wait()
    for i in range(3):
        turned[i] = field[i].T
    edge_cols[:, pl.ds(8, 112), :] = jnp.zeros((3, 112, 128), F32)

    pl.semaphore_wait(barrier, len(neighbours) + cols - 1)

    top, bottom = pl.ds(0, 8), pl.ds(120, 8)
    sends = []

    def send(src, dst, slot, target):
        copy = pltpu.make_async_remote_copy(
            src_ref=src, dst_ref=dst, send_sem=edge_send.at[slot], recv_sem=edge_recv.at[slot],
            device_id=target, device_id_type=MESH,
        )
        copy.start()
        sends.append(copy)

    send(field.at[:, top, :], edge_rows.at[1], 1, (north, c))
    send(field.at[:, bottom, :], edge_rows.at[0], 0, (south, c))
    send(turned.at[:, top, :], edge_cols.at[:, top, :], 6, (r, west))
    send(turned.at[:, bottom, :], edge_cols.at[:, bottom, :], 7, (r, east))
    send(field.at[:, top, :], edge_rows.at[5], 5, (north, west))
    send(field.at[:, top, :], edge_rows.at[4], 4, (north, east))
    send(field.at[:, bottom, :], edge_rows.at[3], 3, (south, west))
    send(field.at[:, bottom, :], edge_rows.at[2], 2, (south, east))

    small_copies[0].wait()
    lane = lax.broadcasted_iota(jnp.int32, (8, 64), 1)
    sub = lax.broadcasted_iota(jnp.int32, (8, 64), 0)
    spread = jnp.where(lane // 8 == sub, flags[...].astype(F32), 0.0)
    from_tile = lax.broadcasted_iota(jnp.int32, (64, 128), 0)
    to_lane = lax.broadcasted_iota(jnp.int32, (64, 128), 1)
    inside = jnp.dot(
        spread, (from_tile % 8 == to_lane // TSIDE).astype(F32), preferred_element_type=F32
    )

    wide_rows, wide_cols = 136, 256
    at_row = lax.broadcasted_iota(jnp.int32, (wide_rows, wide_cols), 0)
    at_col = lax.broadcasted_iota(jnp.int32, (wide_rows, wide_cols), 1)
    low_row = jnp.where(r == rows - 1, 128, 132)
    high_row = jnp.where(r == 0, 136, 132)
    low_col = jnp.where(c == cols - 1, 128, 192)
    high_col = jnp.where(c == 0, 256, 192)
    valid = ((at_row < low_row) | (at_row >= high_row)) & ((at_col < low_col) | (at_col >= high_col))
    upper_half = lax.broadcasted_iota(jnp.int32, (8, 128), 0) < 4
    left_half = lax.broadcasted_iota(jnp.int32, (8, 128), 1) < 64

    for copy in sends:
        copy.wait_recv()

    wide = []
    for i in range(3):
        beside = edge_cols[i].T
        under = jnp.where(upper_half, edge_rows[1, i], edge_rows[0, i])
        corner = jnp.where(
            left_half,
            jnp.where(upper_half, edge_rows[5, i], edge_rows[3, i]),
            jnp.where(upper_half, edge_rows[4, i], edge_rows[2, i]),
        )
        whole = jnp.concatenate(
            [jnp.concatenate([field[i], beside], axis=1), jnp.concatenate([under, corner], axis=1)], axis=0
        )
        wide.append(jnp.where(valid, whole, 0.0))
    start, press, source = wide
    across = (pltpu.roll(press, wide_cols - 1, 1) - press) / 24.0
    down = (pltpu.roll(press, wide_rows - 1, 0) - press) / 24.0
    current = start
    for _ in range(PASSES):
        cubed = current * current * current
        flux_across = (cubed + pltpu.roll(cubed, wide_cols - 1, 1)) * across
        flux_down = (cubed + pltpu.roll(cubed, wide_rows - 1, 0)) * down
        total = (flux_across - pltpu.roll(flux_across, 1, 1)) + (flux_down - pltpu.roll(flux_down, 1, 0))
        current = jnp.where(valid, start + STEP * (total + source), 0.0)
    middle[...] = current[:128, :128]

    own = pl.multiple_of(c * 64, 64)
    rows_of = [middle[pl.ds(i, 8, stride=TSIDE), :] * inside for i in range(TSIDE)]
    for i in range(TSIDE):
        opening_out[pl.ds(i, 8, stride=TSIDE), :] = rows_of[i]
    first, second = swap_blocks(rows_of[:8]), swap_blocks(rows_of[8:])
    for e in range(8):
        near[0, pl.ds(e, 8, stride=8), :] = first[e]
        near[1, pl.ds(e, 8, stride=8), :] = second[e]
    tiles = jnp.concatenate([near[0], near[1]], axis=1)
    band[pl.ds(own, 64), :] = tiles

    band_sends = []
    for step in range(1, cols):
        copy = pltpu.make_async_remote_copy(
            src_ref=band.at[pl.ds(own, 64), :], dst_ref=band.at[pl.ds(own, 64), :],
            send_sem=band_send.at[step], recv_sem=band_recv.at[step],
            device_id=(r, lax.rem(c + step, cols)), device_id_type=MESH,
        )
        copy.start()
        band_sends.append(copy)

    small_copies[1].wait()
    own_term = lax.dot_general(
        tiles, self_kernel[...], (((1,), (1,)), ((), ())), precision=HIGHEST, preferred_element_type=F32
    )
    near[0], near[1] = own_term[:, :128], own_term[:, 128:]
    for copy in small_copies[2:]:
        copy.wait()
    for copy in factor_copies:
        copy.wait()

    at_rank = lax.broadcasted_iota(jnp.int32, (16, 256), 0)

    def cut(t, carry):
        for k in range(4):
            left[t, k] = jnp.where(at_rank < rank[k, t], left[t, k], 0.0)
        return carry

    lax.fori_loop(0, 64, cut, 0)
    for copy in sends:
        copy.wait_send()
    for copy in band_sends:
        copy.wait()

    ones = jnp.ones((256, 128), jnp.bfloat16)
    group = 8

    def interact(g, carry):
        highs, lows = [], []
        for u in range(group):
            t = g * group + u
            for k in range(4):
                at = column[k, t] * 64 + tile[k, t]
                product = right[t, k] * band[pl.ds(at, 1), :]
                high, low = split_bf16(product[:, :128] + product[:, 128:])
                highs.append(high)
                lows.append(low)
        parts = jnp.concatenate([jnp.concatenate(highs, axis=0), jnp.concatenate(lows, axis=0)], axis=1)
        coefficients = jnp.dot(parts, ones, preferred_element_type=F32)
        sums = [[], []]
        for u in range(group):
            t = g * group + u
            factor = left[t].reshape(64, 256)
            scale = coefficients[u * 64:(u + 1) * 64]
            for h in range(2):
                sums[h].append(jnp.sum(factor[:, h * 128:(h + 1) * 128] * scale, axis=0, keepdims=True))
        at = pl.ds(pl.multiple_of(g * group, group), group)
        for h in range(2):
            near[h, at, :] = near[h, at, :] + jnp.concatenate(sums[h], axis=0)
        return carry

    lax.fori_loop(0, 64 // group, interact, 0)

    laid = []
    for h in range(2):
        laid += swap_blocks([near[h, pl.ds(e, 8, stride=8), :] for e in range(8)])
    for i in range(TSIDE):
        pressure_out[pl.ds(i, 8, stride=TSIDE), :] = laid[i]


def local(
    opening_old, pressure_old, injection, front_flags, self_kernel,
    source_column, source_tile, source_rank, left_factor, right_factor,
):
    rows, cols = lax.axis_size("row"), lax.axis_size("col")
    anywhere = pl.BlockSpec(memory_space=pl.ANY)
    out = jax.ShapeDtypeStruct((128, 128), F32)
    lists = [a[0].T for a in (source_column, source_tile, source_rank)]
    dma = pltpu.SemaphoreType.DMA
    return pl.pallas_call(
        functools.partial(kernel, rows, cols),
        out_shape=(out, out),
        in_specs=[anywhere] * 10,
        out_specs=(pl.BlockSpec(memory_space=pltpu.VMEM),) * 2,
        scratch_shapes=[
            pltpu.VMEM((3, 128, 128), F32),
            pltpu.VMEM((3, 128, 128), F32),
            pltpu.VMEM((6, 3, 8, 128), F32),
            pltpu.VMEM((3, 128, 128), F32),
            pltpu.VMEM((128, 128), F32),
            pltpu.VMEM((64 * cols, 256), F32),
            pltpu.VMEM((64, 4, 16, 256), F32),
            pltpu.VMEM((64, 4, 16, 256), F32),
            pltpu.VMEM((256, 256), F32),
            pltpu.VMEM((1, 64), jnp.int32),
            pltpu.VMEM((2, 64, 128), F32),
            pltpu.SMEM((4, 64), jnp.int32),
            pltpu.SMEM((4, 64), jnp.int32),
            pltpu.SMEM((4, 64), jnp.int32),
            dma((3,)),
            dma((5,)),
            dma((2,)),
            dma((8,)),
            dma((8,)),
            dma((16,)),
            dma((16,)),
        ],
        compiler_params=pltpu.CompilerParams(
            collective_id=0, has_side_effects=True, vmem_limit_bytes=58 * 1024 * 1024
        ),
        name="fracture",
    )(opening_old, pressure_old, injection, front_flags, self_kernel, *lists, left_factor[0], right_factor[0])


def solution(mesh):
    fields, lists, factors = P("row", "col"), P("row", "col", None), P("row", "col", None, None, None)
    return jax.shard_map(
        local,
        mesh=mesh,
        in_specs=(fields, fields, fields, fields, P(), lists, lists, lists, factors, factors),
        out_specs=(fields, fields),
        check_vma=False,
    )
```

time: 135 us -> 38 us (0.28)
  waiting for transfers between devices: 59.5 us -> 0 us
  starting transfers between devices: 39.3 us -> 0 us
  Pallas kernels: 0 us -> 34.2 us
  between operations: 14.5 us -> 0.64 us
  matrix products: 8.59 us -> 0 us
  other arithmetic: 6.9 us -> 0 us
  local copies, waits for them, and re-layouts: 5.14 us -> 2.95 us
    all_gather x1 -> x0, waiting for transfers between devices: 53.2 us -> none  [local(): band = lax.all_gather(tile_rows, 'col', axis=0, tiled=True)]
    ppermute x12 -> x0, starting transfers between devices: 39.3 us -> none  [the longest x6 25.6 us: with_halo(): before = lax.ppermute(last, axis, up)]
    pallas_call x0 -> x1, Pallas kernels: none -> 34.2 us  [local(): pl.pallas_call(functools.partial(kernel, rows, cols), out_shape=(out, out...]
    dot_general x3 -> x0, matrix products: 8.59 us -> none  [the longest x1 5.86 us: local(): jnp.einsum('tkjs,tks->tkj', right_factor[0], sources, precision=highest_m...]
    ppermute x12 -> x0, waiting for transfers between devices: 6.35 us -> none  [the longest x6 5.71 us: with_halo(): before = lax.ppermute(last, axis, up)]
    unnamed x18 -> x2, local copies, waits for them, and re-layouts: 0.06 us -> 2.95 us
    gather x1 -> x0, local copies, waits for them, and re-layouts: 2.19 us -> none  [local(): sources = band[columns * tile_count + picks]]
    add x3 -> x0, other arithmetic: 2.17 us -> none  [the longest x2 2.17 us: picard_pass(): return start_open + step_size * (accumulated + inject_part)]
  transfers between devices with their start and end apart: 13 -> 0, of which waited for: 8 -> 0; matrix products, arithmetic and copies ran while one was open for 1% -> 0% of each run, Pallas kernels for 0% -> 0%
where the time goes in v1:
time: 38 us; the launch traced here: 37.8 us
  Pallas kernels  34.2 us (90%)
  local copies, waits for them, and re-layouts  2.95 us (8%)
  between operations  0.64 us (2%)
    pallas_call x1, Pallas kernels, local(): pl.pallas_call(functools.partial(kernel, rows, cols), out_shape=(out, out...  34.2 us
    unnamed x2, local copies, waits for them, and re-layouts  2.95 us

profile of v1, /device:TPU:1, one launch (start us, length us, event | category | flops | bytes accessed | tf_op | source)
XLA Modules:
  0.0 37.8 jit_solution(1290856096895778199)
XLA Ops:
  0.6 34.2 %fracture.1 = (f32[128,128]{1,0:T(8,128)}, f32[128,128]{1,0:T(8,128)}) custom-call(f32[128,128]{1,0:T(8,128)} %opening_ref.1, f32[128,128]{1,0:T(8,128)} %pressure_ref.1, f32[128,128]{1,0:T(8,128)} %injection_ref.1, s32[1,64]{1,0:T(1,128)} %flags_ref.1, f32[256,256]{1,0:T(8,128)} %self_ref.1, s32[4,64]{1,0:T(4,128)} %bitcast.13, s32[4,64]{1,0:T(4,128)} %bitcast.14, ...), custom_call_target="tpu_custom_call" | custom-call | tf_op jit(solution)/shard_map/fracture/pallas_call | solution.py:242
  34.8 1.5 %copy.14 = f32[128,128]{1,0:T(8,128)} copy(f32[128,128]{1,0:T(8,128)} %get-tuple-element.4) | data formatting | bytes 131072
  36.3 1.5 %copy.15 = f32[128,128]{1,0:T(8,128)} copy(f32[128,128]{1,0:T(8,128)} %get-tuple-element.5) | data formatting | bytes 131072

commit v2 on v1

--- a/solution.py
+++ b/solution.py
@@ -35,23 +35,31 @@
     return high, low
 
 
+def flat_tiles(rows_of):
+    return swap_blocks(rows_of[:8]), swap_blocks(rows_of[8:])
+
+
 def kernel(
     rows, cols,
     opening_ref, pressure_ref, injection_ref, flags_ref, self_ref,
     column_ref, tile_ref, rank_ref, left_ref, right_ref,
     opening_out, pressure_out,
-    field, turned, edge_rows, edge_cols, middle, band, left, right, self_kernel, flags, near,
+    field, turned, edge_rows, edge_cols, middle, early, band, patches, left, right, self_kernel, flags, near,
     column, tile, rank,
-    field_sem, small_sem, factor_sem, edge_send, edge_recv, band_send, band_recv,
+    field_sem, small_sem, factor_sem, edge_send, edge_recv, early_send, early_recv, pass_send, pass_recv,
+    patch_send, patch_recv,
 ):
     r, c = lax.axis_index("row"), lax.axis_index("col")
-    north, south = lax.rem(r + rows - 1, rows), lax.rem(r + 1, rows)
     west, east = lax.rem(c + cols - 1, cols), lax.rem(c + 1, cols)
-    neighbours = [(north, c), (south, c), (north, west), (north, east), (south, west), (south, east)]
+    has_north, has_south = r > 0, r < rows - 1
+    north, south = jnp.maximum(r - 1, 0), jnp.minimum(r + 1, rows - 1)
 
     barrier = pltpu.get_barrier_semaphore()
-    for target in neighbours:
-        pl.semaphore_signal(barrier, inc=1, device_id=target, device_id_type=MESH)
+    for there, to in ((has_north, north), (has_south, south)):
+        @pl.when(there)
+        def _():
+            for beside in (c, west, east):
+                pl.semaphore_signal(barrier, inc=1, device_id=(to, beside), device_id_type=MESH)
     for step in range(1, cols):
         pl.semaphore_signal(
             barrier, inc=1, device_id=(r, lax.rem(c + step, cols)), device_id_type=MESH
@@ -79,27 +87,35 @@
         turned[i] = field[i].T
     edge_cols[:, pl.ds(8, 112), :] = jnp.zeros((3, 112, 128), F32)
 
-    pl.semaphore_wait(barrier, len(neighbours) + cols - 1)
-
+    sends, sends_north, sends_south = [], [], []
     top, bottom = pl.ds(0, 8), pl.ds(120, 8)
-    sends = []
-
-    def send(src, dst, slot, target):
-        copy = pltpu.make_async_remote_copy(
+
+    def edge(src, dst, slot, target, to):
+        to.append(pltpu.make_async_remote_copy(
             src_ref=src, dst_ref=dst, send_sem=edge_send.at[slot], recv_sem=edge_recv.at[slot],
             device_id=target, device_id_type=MESH,
-        )
-        copy.start()
-        sends.append(copy)
-
-    send(field.at[:, top, :], edge_rows.at[1], 1, (north, c))
-    send(field.at[:, bottom, :], edge_rows.at[0], 0, (south, c))
-    send(turned.at[:, top, :], edge_cols.at[:, top, :], 6, (r, west))
-    send(turned.at[:, bottom, :], edge_cols.at[:, bottom, :], 7, (r, east))
-    send(field.at[:, top, :], edge_rows.at[5], 5, (north, west))
-    send(field.at[:, top, :], edge_rows.at[4], 4, (north, east))
-    send(field.at[:, bottom, :], edge_rows.at[3], 3, (south, west))
-    send(field.at[:, bottom, :], edge_rows.at[2], 2, (south, east))
+        ))
+
+    edge(field.at[:, top, :], edge_rows.at[1], 1, (north, c), sends_north)
+    edge(field.at[:, top, :], edge_rows.at[5], 5, (north, west), sends_north)
+    edge(field.at[:, top, :], edge_rows.at[4], 4, (north, east), sends_north)
+    edge(field.at[:, bottom, :], edge_rows.at[0], 0, (south, c), sends_south)
+    edge(field.at[:, bottom, :], edge_rows.at[3], 3, (south, west), sends_south)
+    edge(field.at[:, bottom, :], edge_rows.at[2], 2, (south, east), sends_south)
+    edge(turned.at[:, top, :], edge_cols.at[:, top, :], 6, (r, west), sends)
+    edge(turned.at[:, bottom, :], edge_cols.at[:, bottom, :], 7, (r, east), sends)
+
+    pl.semaphore_wait(
+        barrier, 3 * has_north.astype(jnp.int32) + 3 * has_south.astype(jnp.int32) + cols - 1
+    )
+
+    for there, group in ((has_north, sends_north), (has_south, sends_south)):
+        @pl.when(there)
+        def _():
+            for copy in group:
+                copy.start()
+    for copy in sends:
+        copy.start()
 
     small_copies[0].wait()
     lane = lax.broadcasted_iota(jnp.int32, (8, 64), 1)
@@ -110,6 +126,40 @@
     inside = jnp.dot(
         spread, (from_tile % 8 == to_lane // TSIDE).astype(F32), preferred_element_type=F32
     )
+
+    def passes(start, press, source, keep):
+        height, width = start.shape
+        across = (pltpu.roll(press, width - 1, 1) - press) / 24.0
+        down = (pltpu.roll(press, height - 1, 0) - press) / 24.0
+        current = start
+        for _ in range(PASSES):
+            cubed = current * current * current
+            flux_across = (cubed + pltpu.roll(cubed, width - 1, 1)) * across
+            flux_down = (cubed + pltpu.roll(cubed, height - 1, 0)) * down
+            total = (flux_across - pltpu.roll(flux_across, 1, 1)) + (flux_down - pltpu.roll(flux_down, 1, 0))
+            current = keep(start + STEP * (total + source))
+        return current
+
+    middle[...] = passes(field[0], field[1], field[2], lambda v: v)
+    first, second = flat_tiles([middle[pl.ds(i, 8, stride=TSIDE), :] * inside for i in range(TSIDE)])
+    for e in range(8):
+        early[0, pl.ds(e, 8, stride=8), :] = first[e]
+        early[1, pl.ds(e, 8, stride=8), :] = second[e]
+
+    def block(of):
+        return band.at[:, pl.ds(pl.multiple_of(of * 64, 64), 64), :]
+
+    sibling = (r, c ^ 1)
+    chips = (4, 5, 3, 7, 1, 2, 6)
+    early_sends = [
+        pltpu.make_async_remote_copy(
+            src_ref=early, dst_ref=block(c), send_sem=early_send.at[i], recv_sem=early_recv.at[i],
+            device_id=sibling if i == 0 else (r, c ^ (2 * i)), device_id_type=MESH,
+        )
+        for i in chips + (0,)
+    ]
+    for copy in early_sends:
+        copy.start()
 
     wide_rows, wide_cols = 136, 256
     at_row = lax.broadcasted_iota(jnp.int32, (wide_rows, wide_cols), 0)
@@ -122,6 +172,11 @@
     upper_half = lax.broadcasted_iota(jnp.int32, (8, 128), 0) < 4
     left_half = lax.broadcasted_iota(jnp.int32, (8, 128), 1) < 64
 
+    for there, group in ((has_south, sends_north), (has_north, sends_south)):
+        @pl.when(there)
+        def _():
+            for copy in group:
+                copy.wait_recv()
     for copy in sends:
         copy.wait_recv()
 
@@ -138,42 +193,52 @@
             [jnp.concatenate([field[i], beside], axis=1), jnp.concatenate([under, corner], axis=1)], axis=0
         )
         wide.append(jnp.where(valid, whole, 0.0))
-    start, press, source = wide
-    across = (pltpu.roll(press, wide_cols - 1, 1) - press) / 24.0
-    down = (pltpu.roll(press, wide_rows - 1, 0) - press) / 24.0
-    current = start
-    for _ in range(PASSES):
-        cubed = current * current * current
-        flux_across = (cubed + pltpu.roll(cubed, wide_cols - 1, 1)) * across
-        flux_down = (cubed + pltpu.roll(cubed, wide_rows - 1, 0)) * down
-        total = (flux_across - pltpu.roll(flux_across, 1, 1)) + (flux_down - pltpu.roll(flux_down, 1, 0))
-        current = jnp.where(valid, start + STEP * (total + source), 0.0)
+    current = passes(*wide, lambda v: jnp.where(valid, v, 0.0))
     middle[...] = current[:128, :128]
 
     own = pl.multiple_of(c * 64, 64)
     rows_of = [middle[pl.ds(i, 8, stride=TSIDE), :] * inside for i in range(TSIDE)]
+    first, second = flat_tiles(rows_of)
+    for e in range(8):
+        band[0, pl.ds(own + e, 8, stride=8), :] = first[e]
+        band[1, pl.ds(own + e, 8, stride=8), :] = second[e]
+
+    at_lane = lax.broadcasted_iota(jnp.int32, (8, 128), 1)
+    in_row = at_lane % TSIDE
+    left_edge, right_edge = in_row < PASSES, in_row >= TSIDE - PASSES
+    outer = left_edge | right_edge
+    ends = [jnp.where(in_row < TSIDE // 2, half[0], half[7]) for half in (first, second)]
+    patches[c, 0] = jnp.where(outer, ends[0], pltpu.roll(ends[1], 6, 1))
+    patches[c, 1] = jnp.where(
+        left_half, band[0, pl.ds(own, 8), :], band[1, pl.ds(pl.multiple_of(own + 56, 8), 8), :]
+    )
+    patch_sends = []
+    for step in range(1, cols):
+        copy = pltpu.make_async_remote_copy(
+            src_ref=patches.at[c], dst_ref=patches.at[c],
+            send_sem=patch_send.at[step], recv_sem=patch_recv.at[step],
+            device_id=(r, lax.rem(c + step, cols)), device_id_type=MESH,
+        )
+        copy.start()
+        patch_sends.append(copy)
     for i in range(TSIDE):
         opening_out[pl.ds(i, 8, stride=TSIDE), :] = rows_of[i]
-    first, second = swap_blocks(rows_of[:8]), swap_blocks(rows_of[8:])
-    for e in range(8):
-        near[0, pl.ds(e, 8, stride=8), :] = first[e]
-        near[1, pl.ds(e, 8, stride=8), :] = second[e]
-    tiles = jnp.concatenate([near[0], near[1]], axis=1)
-    band[pl.ds(own, 64), :] = tiles
-
-    band_sends = []
-    for step in range(1, cols):
+
+    passed = []
+    for n, i in enumerate(chips):
+        early_sends[n].wait_recv()
         copy = pltpu.make_async_remote_copy(
-            src_ref=band.at[pl.ds(own, 64), :], dst_ref=band.at[pl.ds(own, 64), :],
-            send_sem=band_send.at[step], recv_sem=band_recv.at[step],
-            device_id=(r, lax.rem(c + step, cols)), device_id_type=MESH,
-        )
-        copy.start()
-        band_sends.append(copy)
+            src_ref=block(c ^ (2 * i)), dst_ref=block(c ^ (2 * i)),
+            send_sem=pass_send.at[i], recv_sem=pass_recv.at[i],
+            device_id=sibling, device_id_type=MESH,
+        )
+        copy.start()
+        passed.append(copy)
 
     small_copies[1].wait()
+    own_tiles = jnp.concatenate([band[h, pl.ds(own, 64), :] for h in range(2)], axis=1)
     own_term = lax.dot_general(
-        tiles, self_kernel[...], (((1,), (1,)), ((), ())), precision=HIGHEST, preferred_element_type=F32
+        own_tiles, self_kernel[...], (((1,), (1,)), ((), ())), precision=HIGHEST, preferred_element_type=F32
     )
     near[0], near[1] = own_term[:, :128], own_term[:, 128:]
     for copy in small_copies[2:]:
@@ -189,10 +254,35 @@
         return carry
 
     lax.fori_loop(0, 64, cut, 0)
-    for copy in sends:
+    for there, group in ((has_north, sends_north), (has_south, sends_south)):
+        @pl.when(there)
+        def _():
+            for copy in group:
+                copy.wait_send()
+    for copy in sends + early_sends + patch_sends:
         copy.wait_send()
-    for copy in band_sends:
+    early_sends[-1].wait_recv()
+    for copy in passed:
         copy.wait()
+    for copy in patch_sends:
+        copy.wait_recv()
+
+    def patch(step, carry):
+        of = lax.rem(c + step, cols)
+        base = pl.multiple_of(of * 64, 64)
+        columns = patches[of, 0]
+        for h, value in ((0, columns), (1, pltpu.roll(columns, 122, 1))):
+            for start, mask in ((base, left_edge), (base + 7, right_edge)):
+                at = pl.ds(start, 8, stride=8)
+                band[h, at, :] = jnp.where(mask, value, band[h, at, :])
+        for h, start, mask in (
+            (0, base, at_lane < PASSES * TSIDE), (1, base + 56, at_lane >= 128 - PASSES * TSIDE)
+        ):
+            at = pl.ds(pl.multiple_of(start, 8), 8)
+            band[h, at, :] = jnp.where(mask, patches[of, 1], band[h, at, :])
+        return carry
+
+    lax.fori_loop(1, cols, patch, 0)
 
     ones = jnp.ones((256, 128), jnp.bfloat16)
     group = 8
@@ -203,8 +293,10 @@
             t = g * group + u
             for k in range(4):
                 at = column[k, t] * 64 + tile[k, t]
-                product = right[t, k] * band[pl.ds(at, 1), :]
-                high, low = split_bf16(product[:, :128] + product[:, 128:])
+                factor = right[t, k]
+                high, low = split_bf16(
+                    factor[:, :128] * band[0, pl.ds(at, 1), :] + factor[:, 128:] * band[1, pl.ds(at, 1), :]
+                )
                 highs.append(high)
                 lows.append(low)
         parts = jnp.concatenate([jnp.concatenate(highs, axis=0), jnp.concatenate(lows, axis=0)], axis=1)
@@ -250,7 +342,9 @@
             pltpu.VMEM((6, 3, 8, 128), F32),
             pltpu.VMEM((3, 128, 128), F32),
             pltpu.VMEM((128, 128), F32),
-            pltpu.VMEM((64 * cols, 256), F32),
+            pltpu.VMEM((2, 64, 128), F32),
+            pltpu.VMEM((2, 64 * cols, 128), F32),
+            pltpu.VMEM((cols, 2, 8, 128), F32),
             pltpu.VMEM((64, 4, 16, 256), F32),
             pltpu.VMEM((64, 4, 16, 256), F32),
             pltpu.VMEM((256, 256), F32),
@@ -264,6 +358,10 @@
             dma((2,)),
             dma((8,)),
             dma((8,)),
+            dma((8,)),
+            dma((8,)),
+            dma((8,)),
+            dma((8,)),
             dma((16,)),
             dma((16,)),
         ],

time: 38 us -> 25.9 us (0.68)
  the two profiles are of different devices: /device:TPU:1 before, /device:TPU:193 now
where the time goes in v2:
time: 25.9 us; the launch traced here: 25.7 us
  Pallas kernels  22.2 us (86%)
  local copies, waits for them, and re-layouts  2.95 us (11%)
  between operations  0.64 us (2%)
    pallas_call x1, Pallas kernels, local(): pl.pallas_call(functools.partial(kernel, rows, cols), out_shape=(out, out...  22.2 us
    unnamed x2, local copies, waits for them, and re-layouts  2.95 us

profile of v2, /device:TPU:193, one launch (start us, length us, event | category | flops | bytes accessed | tf_op | source)
XLA Modules:
  0.0 25.7 jit_solution(3855158583777577825)
XLA Ops:
  0.6 22.2 %fracture.1 = (f32[128,128]{1,0:T(8,128)}, f32[128,128]{1,0:T(8,128)}) custom-call(f32[128,128]{1,0:T(8,128)} %opening_ref.1, f32[128,128]{1,0:T(8,128)} %pressure_ref.1, f32[128,128]{1,0:T(8,128)} %injection_ref.1, s32[1,64]{1,0:T(1,128)} %flags_ref.1, f32[256,256]{1,0:T(8,128)} %self_ref.1, s32[4,64]{1,0:T(4,128)} %bitcast.13, s32[4,64]{1,0:T(4,128)} %bitcast.14, ...), custom_call_target="tpu_custom_call" | custom-call | tf_op jit(solution)/shard_map/fracture/pallas_call | solution.py:334
  22.8 1.5 %copy.14 = f32[128,128]{1,0:T(8,128)} copy(f32[128,128]{1,0:T(8,128)} %get-tuple-element.4) | data formatting | bytes 131072
  24.3 1.5 %copy.15 = f32[128,128]{1,0:T(8,128)} copy(f32[128,128]{1,0:T(8,128)} %get-tuple-element.5) | data formatting | bytes 131072

commit v3 on v2

--- a/solution.py
+++ b/solution.py
@@ -44,7 +44,7 @@
     opening_ref, pressure_ref, injection_ref, flags_ref, self_ref,
     column_ref, tile_ref, rank_ref, left_ref, right_ref,
     opening_out, pressure_out,
-    field, turned, edge_rows, edge_cols, middle, early, band, patches, left, right, self_kernel, flags, near,
+    field, turned, from_side, edge_rows, edge_cols, middle, early, band, patches, left, right, self_kernel, flags, near,
     column, tile, rank,
     field_sem, small_sem, factor_sem, edge_send, edge_recv, early_send, early_recv, pass_send, pass_recv,
     patch_send, patch_recv,
@@ -53,6 +53,23 @@
     west, east = lax.rem(c + cols - 1, cols), lax.rem(c + 1, cols)
     has_north, has_south = r > 0, r < rows - 1
     north, south = jnp.maximum(r - 1, 0), jnp.minimum(r + 1, rows - 1)
+
+    field_copies = [
+        pltpu.make_async_copy(ref, field.at[i], field_sem.at[i])
+        for i, ref in enumerate((opening_ref, pressure_ref, injection_ref))
+    ]
+    small_copies = [
+        pltpu.make_async_copy(ref, to, small_sem.at[i])
+        for i, (ref, to) in enumerate(
+            ((flags_ref, flags), (self_ref, self_kernel), (column_ref, column), (tile_ref, tile), (rank_ref, rank))
+        )
+    ]
+    factor_copies = [
+        pltpu.make_async_copy(right_ref, right, factor_sem.at[0]),
+        pltpu.make_async_copy(left_ref, left, factor_sem.at[1]),
+    ]
+    for copy in field_copies + small_copies:
+        copy.start()
 
     barrier = pltpu.get_barrier_semaphore()
     for there, to in ((has_north, north), (has_south, south)):
@@ -65,22 +82,6 @@
             barrier, inc=1, device_id=(r, lax.rem(c + step, cols)), device_id_type=MESH
         )
 
-    field_copies = [
-        pltpu.make_async_copy(ref, field.at[i], field_sem.at[i])
-        for i, ref in enumerate((opening_ref, pressure_ref, injection_ref))
-    ]
-    small_copies = [
-        pltpu.make_async_copy(ref, to, small_sem.at[i])
-        for i, (ref, to) in enumerate(
-            ((flags_ref, flags), (self_ref, self_kernel), (column_ref, column), (tile_ref, tile), (rank_ref, rank))
-        )
-    ]
-    factor_copies = [
-        pltpu.make_async_copy(right_ref, right, factor_sem.at[0]),
-        pltpu.make_async_copy(left_ref, left, factor_sem.at[1]),
-    ]
-    for copy in field_copies + small_copies + factor_copies:
-        copy.start()
     for copy in field_copies:
         copy.wait()
     for i in range(3):
@@ -96,12 +97,12 @@
             device_id=target, device_id_type=MESH,
         ))
 
-    edge(field.at[:, top, :], edge_rows.at[1], 1, (north, c), sends_north)
     edge(field.at[:, top, :], edge_rows.at[5], 5, (north, west), sends_north)
     edge(field.at[:, top, :], edge_rows.at[4], 4, (north, east), sends_north)
-    edge(field.at[:, bottom, :], edge_rows.at[0], 0, (south, c), sends_south)
+    edge(field.at[:, top, :], edge_rows.at[1], 1, (north, c), sends_north)
     edge(field.at[:, bottom, :], edge_rows.at[3], 3, (south, west), sends_south)
     edge(field.at[:, bottom, :], edge_rows.at[2], 2, (south, east), sends_south)
+    edge(field.at[:, bottom, :], edge_rows.at[0], 0, (south, c), sends_south)
     edge(turned.at[:, top, :], edge_cols.at[:, top, :], 6, (r, west), sends)
     edge(turned.at[:, bottom, :], edge_cols.at[:, bottom, :], 7, (r, east), sends)
 
@@ -158,7 +159,7 @@
         )
         for i in chips + (0,)
     ]
-    for copy in early_sends:
+    for copy in early_sends + factor_copies:
         copy.start()
 
     wide_rows, wide_cols = 136, 256
@@ -172,17 +173,17 @@
     upper_half = lax.broadcasted_iota(jnp.int32, (8, 128), 0) < 4
     left_half = lax.broadcasted_iota(jnp.int32, (8, 128), 1) < 64
 
+    for copy in sends:
+        copy.wait_recv()
+    for i in range(3):
+        from_side[i] = edge_cols[i].T
     for there, group in ((has_south, sends_north), (has_north, sends_south)):
         @pl.when(there)
         def _():
             for copy in group:
                 copy.wait_recv()
-    for copy in sends:
-        copy.wait_recv()
-
     wide = []
     for i in range(3):
-        beside = edge_cols[i].T
         under = jnp.where(upper_half, edge_rows[1, i], edge_rows[0, i])
         corner = jnp.where(
             left_half,
@@ -190,7 +191,7 @@
             jnp.where(upper_half, edge_rows[4, i], edge_rows[2, i]),
         )
         whole = jnp.concatenate(
-            [jnp.concatenate([field[i], beside], axis=1), jnp.concatenate([under, corner], axis=1)], axis=0
+            [jnp.concatenate([field[i], from_side[i]], axis=1), jnp.concatenate([under, corner], axis=1)], axis=0
         )
         wide.append(jnp.where(valid, whole, 0.0))
     current = passes(*wide, lambda v: jnp.where(valid, v, 0.0))
@@ -213,11 +214,11 @@
         left_half, band[0, pl.ds(own, 8), :], band[1, pl.ds(pl.multiple_of(own + 56, 8), 8), :]
     )
     patch_sends = []
-    for step in range(1, cols):
+    for step in (10, 11, 6, 7, 14, 15, 8, 9, 4, 5, 12, 13, 2, 3, 1):
         copy = pltpu.make_async_remote_copy(
             src_ref=patches.at[c], dst_ref=patches.at[c],
             send_sem=patch_send.at[step], recv_sem=patch_recv.at[step],
-            device_id=(r, lax.rem(c + step, cols)), device_id_type=MESH,
+            device_id=(r, c ^ step), device_id_type=MESH,
         )
         copy.start()
         patch_sends.append(copy)
@@ -285,7 +286,7 @@
     lax.fori_loop(1, cols, patch, 0)
 
     ones = jnp.ones((256, 128), jnp.bfloat16)
-    group = 8
+    group = 32
 
     def interact(g, carry):
         highs, lows = [], []
@@ -330,6 +331,7 @@
     anywhere = pl.BlockSpec(memory_space=pl.ANY)
     out = jax.ShapeDtypeStruct((128, 128), F32)
     lists = [a[0].T for a in (source_column, source_tile, source_rank)]
+    operands = (opening_old, pressure_old, injection, front_flags, self_kernel, *lists, left_factor[0], right_factor[0])
     dma = pltpu.SemaphoreType.DMA
     return pl.pallas_call(
         functools.partial(kernel, rows, cols),
@@ -337,6 +339,7 @@
         in_specs=[anywhere] * 10,
         out_specs=(pl.BlockSpec(memory_space=pltpu.VMEM),) * 2,
         scratch_shapes=[
+            pltpu.VMEM((3, 128, 128), F32),
             pltpu.VMEM((3, 128, 128), F32),
             pltpu.VMEM((3, 128, 128), F32),
             pltpu.VMEM((6, 3, 8, 128), F32),
@@ -366,10 +369,10 @@
             dma((16,)),
         ],
         compiler_params=pltpu.CompilerParams(
-            collective_id=0, has_side_effects=True, vmem_limit_bytes=58 * 1024 * 1024
+            collective_id=0, has_side_effects=True, vmem_limit_bytes=40 * 1024 * 1024
         ),
         name="fracture",
-    )(opening_old, pressure_old, injection, front_flags, self_kernel, *lists, left_factor[0], right_factor[0])
+    )(*[pltpu.with_memory_space_constraint(a, pltpu.HBM) for a in operands])
 
 
 def solution(mesh):

time: 25.9 us -> 22.5 us (0.87)
  Pallas kernels: 22.2 us -> 20.5 us
  local copies, waits for them, and re-layouts: 2.95 us -> 1.26 us
    unnamed x2, local copies, waits for them, and re-layouts: 2.95 us -> 1.26 us
    pallas_call x1, Pallas kernels: 22.2 us -> 20.5 us  [local(): pl.pallas_call(functools.partial(kernel, rows, cols), out_shape=(out, out...]
where the time goes in v3:
time: 22.5 us; the launch traced here: 22.4 us
  Pallas kernels  20.5 us (91%)
  local copies, waits for them, and re-layouts  1.26 us (6%)
  between operations  0.64 us (3%)
    pallas_call x1, Pallas kernels, local(): pl.pallas_call(functools.partial(kernel, rows, cols), out_shape=(out, out...  20.5 us
    unnamed x2, local copies, waits for them, and re-layouts  1.26 us

profile of v3, /device:TPU:193, one launch (start us, length us, event | category | flops | bytes accessed | tf_op | source)
XLA Modules:
  0.0 22.4 jit_solution(17113471078195158334)
XLA Ops:
  0.6 20.5 %fracture.1 = (f32[128,128]{1,0:T(8,128)S(1)}, f32[128,128]{1,0:T(8,128)S(1)}) custom-call(f32[128,128]{1,0:T(8,128)} %opening_ref.1, f32[128,128]{1,0:T(8,128)} %pressure_ref.1, f32[128,128]{1,0:T(8,128)} %injection_ref.1, s32[1,64]{1,0:T(1,128)} %flags_ref.1, f32[256,256]{1,0:T(8,128)} %self_ref.1, s32[4,64]{1,0:T(4,128)} %bitcast.13, s32[4,64]{1,0:T(4,128)} %bitcast.14, ...), custom_call_target="tpu_custom_call" | custom-call | tf_op jit(solution)/shard_map/fracture/pallas_call | solution.py:336
  21.1 0.6 %copy.14 = f32[128,128]{1,0:T(8,128)} copy(f32[128,128]{1,0:T(8,128)S(1)} %get-tuple-element.4) | data formatting | bytes 131072
  21.8 0.6 %copy.15 = f32[128,128]{1,0:T(8,128)} copy(f32[128,128]{1,0:T(8,128)S(1)} %get-tuple-element.5) | data formatting | bytes 131072

commit v4 on v3

--- a/solution.py
+++ b/solution.py
@@ -283,7 +283,7 @@
             band[h, at, :] = jnp.where(mask, patches[of, 1], band[h, at, :])
         return carry
 
-    lax.fori_loop(1, cols, patch, 0)
+    lax.fori_loop(1, cols, patch, 0, unroll=15)
 
     ones = jnp.ones((256, 128), jnp.bfloat16)
     group = 32

time: 22.5 us -> 21.5 us (0.956)
  Pallas kernels: 20.5 us -> 19.5 us
    pallas_call x1, Pallas kernels: 20.5 us -> 19.5 us  [local(): pl.pallas_call(functools.partial(kernel, rows, cols), out_shape=(out, out...]
where the time goes in v4:
time: 21.5 us; the launch traced here: 21.4 us
  Pallas kernels  19.5 us (91%)
  local copies, waits for them, and re-layouts  1.26 us (6%)
  between operations  0.64 us (3%)
    pallas_call x1, Pallas kernels, local(): pl.pallas_call(functools.partial(kernel, rows, cols), out_shape=(out, out...  19.5 us
    unnamed x2, local copies, waits for them, and re-layouts  1.26 us

profile of v4, /device:TPU:193, one launch (start us, length us, event | category | flops | bytes accessed | tf_op | source)
XLA Modules:
  0.0 21.4 jit_solution(17264164982945205520)
XLA Ops:
  0.6 19.5 %fracture.1 = (f32[128,128]{1,0:T(8,128)S(1)}, f32[128,128]{1,0:T(8,128)S(1)}) custom-call(f32[128,128]{1,0:T(8,128)} %opening_ref.1, f32[128,128]{1,0:T(8,128)} %pressure_ref.1, f32[128,128]{1,0:T(8,128)} %injection_ref.1, s32[1,64]{1,0:T(1,128)} %flags_ref.1, f32[256,256]{1,0:T(8,128)} %self_ref.1, s32[4,64]{1,0:T(4,128)} %bitcast.13, s32[4,64]{1,0:T(4,128)} %bitcast.14, ...), custom_call_target="tpu_custom_call" | custom-call | tf_op jit(solution)/shard_map/fracture/pallas_call | solution.py:336
  20.2 0.6 %copy.14 = f32[128,128]{1,0:T(8,128)} copy(f32[128,128]{1,0:T(8,128)S(1)} %get-tuple-element.4) | data formatting | bytes 131072
  20.8 0.6 %copy.15 = f32[128,128]{1,0:T(8,128)} copy(f32[128,128]{1,0:T(8,128)S(1)} %get-tuple-element.5) | data formatting | bytes 131072

commit v5 on v4

--- a/solution.py
+++ b/solution.py
@@ -43,7 +43,7 @@
     rows, cols,
     opening_ref, pressure_ref, injection_ref, flags_ref, self_ref,
     column_ref, tile_ref, rank_ref, left_ref, right_ref,
-    opening_out, pressure_out,
+    results,
     field, turned, from_side, edge_rows, edge_cols, middle, early, band, patches, left, right, self_kernel, flags, near,
     column, tile, rank,
     field_sem, small_sem, factor_sem, edge_send, edge_recv, early_send, early_recv, pass_send, pass_recv,
@@ -223,7 +223,7 @@
         copy.start()
         patch_sends.append(copy)
     for i in range(TSIDE):
-        opening_out[pl.ds(i, 8, stride=TSIDE), :] = rows_of[i]
+        results[0, pl.ds(i, 8, stride=TSIDE), :] = rows_of[i]
 
     passed = []
     for n, i in enumerate(chips):
@@ -320,7 +320,7 @@
     for h in range(2):
         laid += swap_blocks([near[h, pl.ds(e, 8, stride=8), :] for e in range(8)])
     for i in range(TSIDE):
-        pressure_out[pl.ds(i, 8, stride=TSIDE), :] = laid[i]
+        results[1, pl.ds(i, 8, stride=TSIDE), :] = laid[i]
 
 
 def local(
@@ -329,15 +329,15 @@
 ):
     rows, cols = lax.axis_size("row"), lax.axis_size("col")
     anywhere = pl.BlockSpec(memory_space=pl.ANY)
-    out = jax.ShapeDtypeStruct((128, 128), F32)
+    out = jax.ShapeDtypeStruct((2, 128, 128), F32)
     lists = [a[0].T for a in (source_column, source_tile, source_rank)]
     operands = (opening_old, pressure_old, injection, front_flags, self_kernel, *lists, left_factor[0], right_factor[0])
     dma = pltpu.SemaphoreType.DMA
-    return pl.pallas_call(
+    both = pl.pallas_call(
         functools.partial(kernel, rows, cols),
-        out_shape=(out, out),
+        out_shape=out,
         in_specs=[anywhere] * 10,
-        out_specs=(pl.BlockSpec(memory_space=pltpu.VMEM),) * 2,
+        out_specs=pl.BlockSpec(memory_space=pltpu.VMEM),
         scratch_shapes=[
             pltpu.VMEM((3, 128, 128), F32),
             pltpu.VMEM((3, 128, 128), F32),
@@ -373,6 +373,7 @@
         ),
         name="fracture",
     )(*[pltpu.with_memory_space_constraint(a, pltpu.HBM) for a in operands])
+    return both[0], both[1]
 
 
 def solution(mesh):

time: 21.5 us -> 20.9 us (0.972)
  local copies, waits for them, and re-layouts: 1.26 us -> 0.66 us
    unnamed x2 -> x0, local copies, waits for them, and re-layouts: 1.26 us -> none
    squeeze x0 -> x1, local copies, waits for them, and re-layouts: none -> 0.66 us  [local(): return (both[0], both[1])]
where the time goes in v5:
time: 20.9 us; the launch traced here: 20.8 us
  Pallas kernels  19.5 us (93%)
  local copies, waits for them, and re-layouts  0.66 us (3%)
  between operations  0.64 us (3%)
    pallas_call x1, Pallas kernels, local(): pl.pallas_call(functools.partial(kernel, rows, cols), out_shape=out, in_s...  19.5 us
    squeeze x1, local copies, waits for them, and re-layouts, local(): return (both[0], both[1])  0.66 us

profile of v5, /device:TPU:193, one launch (start us, length us, event | category | flops | bytes accessed | tf_op | source)
XLA Modules:
  0.0 20.8 jit_solution(9506907988219957787)
XLA Ops:
  0.6 19.5 %fracture.1 = f32[2,128,128]{2,1,0:T(8,128)S(1)} custom-call(f32[128,128]{1,0:T(8,128)} %opening_ref.1, f32[128,128]{1,0:T(8,128)} %pressure_ref.1, f32[128,128]{1,0:T(8,128)} %injection_ref.1, s32[1,64]{1,0:T(1,128)} %flags_ref.1, f32[256,256]{1,0:T(8,128)} %self_ref.1, s32[4,64]{1,0:T(4,128)} %bitcast.17, s32[4,64]{1,0:T(4,128)} %bitcast.18, ...), custom_call_target="tpu_custom_call" | custom-call | tf_op jit(solution)/shard_map/fracture/pallas_call | solution.py:336
  20.2 0.7 %slice_bitcast_fusion = (f32[128,128]{1,0:T(8,128)}, f32[128,128]{1,0:T(8,128)}) fusion(f32[2,128,128]{2,1,0:T(8,128)S(1)} %fracture.1), kind=kLoop, calls=%fused_computation | loop fusion | bytes 262144 | tf_op jit(solution)/shard_map/squeeze | solution.py:376

commit v6 on v5

--- a/solution.py
+++ b/solution.py
@@ -106,18 +106,6 @@
     edge(turned.at[:, top, :], edge_cols.at[:, top, :], 6, (r, west), sends)
     edge(turned.at[:, bottom, :], edge_cols.at[:, bottom, :], 7, (r, east), sends)
 
-    pl.semaphore_wait(
-        barrier, 3 * has_north.astype(jnp.int32) + 3 * has_south.astype(jnp.int32) + cols - 1
-    )
-
-    for there, group in ((has_north, sends_north), (has_south, sends_south)):
-        @pl.when(there)
-        def _():
-            for copy in group:
-                copy.start()
-    for copy in sends:
-        copy.start()
-
     small_copies[0].wait()
     lane = lax.broadcasted_iota(jnp.int32, (8, 64), 1)
     sub = lax.broadcasted_iota(jnp.int32, (8, 64), 0)
@@ -159,7 +147,24 @@
         )
         for i in chips + (0,)
     ]
-    for copy in early_sends + factor_copies:
+    pl.semaphore_wait(
+        barrier, 3 * has_north.astype(jnp.int32) + 3 * has_south.astype(jnp.int32) + cols - 1
+    )
+
+    for there, group in ((has_north, sends_north), (has_south, sends_south)):
+        @pl.when(there)
+        def _():
+            for copy in group:
+                copy.start()
+    for copy in sends:
+        copy.start()
+
+    for core, order in ((0, (4, 5, 3, 7, 1, 2, 6, 0)), (1, (5, 3, 4, 7, 2, 1, 6, 0))):
+        @pl.when(lax.rem(c, 2) == core)
+        def _():
+            for i in order:
+                early_sends[chips.index(i) if i else 7].start()
+    for copy in factor_copies:
         copy.start()
 
     wide_rows, wide_cols = 136, 256
@@ -286,7 +291,7 @@
     lax.fori_loop(1, cols, patch, 0, unroll=15)
 
     ones = jnp.ones((256, 128), jnp.bfloat16)
-    group = 32
+    group = 64
 
     def interact(g, carry):
         highs, lows = [], []

time: 20.9 us -> 20.9 us (level)
  no operation moved by 1% of the time
where the time goes in v6:
time: 20.9 us; the launch traced here: 20.8 us
  Pallas kernels  19.5 us (93%)
  local copies, waits for them, and re-layouts  0.66 us (3%)
  between operations  0.64 us (3%)
    pallas_call x1, Pallas kernels, local(): pl.pallas_call(functools.partial(kernel, rows, cols), out_shape=out, in_s...  19.5 us
    squeeze x1, local copies, waits for them, and re-layouts, local(): return (both[0], both[1])  0.66 us

profile of v6, /device:TPU:193, one launch (start us, length us, event | category | flops | bytes accessed | tf_op | source)
XLA Modules:
  0.0 20.8 jit_solution(9207354690569702268)
XLA Ops:
  0.6 19.5 %fracture.1 = f32[2,128,128]{2,1,0:T(8,128)S(1)} custom-call(f32[128,128]{1,0:T(8,128)} %opening_ref.1, f32[128,128]{1,0:T(8,128)} %pressure_ref.1, f32[128,128]{1,0:T(8,128)} %injection_ref.1, s32[1,64]{1,0:T(1,128)} %flags_ref.1, f32[256,256]{1,0:T(8,128)} %self_ref.1, s32[4,64]{1,0:T(4,128)} %bitcast.17, s32[4,64]{1,0:T(4,128)} %bitcast.18, ...), custom_call_target="tpu_custom_call" | custom-call | tf_op jit(solution)/shard_map/fracture/pallas_call | solution.py:341
  20.1 0.7 %slice_bitcast_fusion = (f32[128,128]{1,0:T(8,128)}, f32[128,128]{1,0:T(8,128)}) fusion(f32[2,128,128]{2,1,0:T(8,128)S(1)} %fracture.1), kind=kLoop, calls=%fused_computation | loop fusion | bytes 262144 | tf_op jit(solution)/shard_map/squeeze | solution.py:381

commit v7 on v6

--- a/solution.py
+++ b/solution.py
@@ -267,14 +267,10 @@
                 copy.wait_send()
     for copy in sends + early_sends + patch_sends:
         copy.wait_send()
-    early_sends[-1].wait_recv()
-    for copy in passed:
-        copy.wait()
     for copy in patch_sends:
         copy.wait_recv()
 
-    def patch(step, carry):
-        of = lax.rem(c + step, cols)
+    def patch(of):
         base = pl.multiple_of(of * 64, 64)
         columns = patches[of, 0]
         for h, value in ((0, columns), (1, pltpu.roll(columns, 122, 1))):
@@ -286,9 +282,15 @@
         ):
             at = pl.ds(pl.multiple_of(start, 8), 8)
             band[h, at, :] = jnp.where(mask, patches[of, 1], band[h, at, :])
-        return carry
-
-    lax.fori_loop(1, cols, patch, 0, unroll=15)
+
+    for i, copy in zip(chips, passed):
+        copy.wait_send()
+        patch(c ^ (2 * i))
+    early_sends[-1].wait_recv()
+    patch(c ^ 1)
+    for i, copy in zip(chips, passed):
+        copy.wait_recv()
+        patch(c ^ (2 * i) ^ 1)
 
     ones = jnp.ones((256, 128), jnp.bfloat16)
     group = 64

time: 20.9 us -> 21.8 us (1.043)
  Pallas kernels: 19.5 us -> 20.4 us
    pallas_call x1, Pallas kernels: 19.5 us -> 20.4 us  [local(): pl.pallas_call(functools.partial(kernel, rows, cols), out_shape=out, in_s...]
where the time goes in v7:
time: 21.8 us; the launch traced here: 21.7 us
  Pallas kernels  20.4 us (94%)
  local copies, waits for them, and re-layouts  0.66 us (3%)
  between operations  0.64 us (3%)
    pallas_call x1, Pallas kernels, local(): pl.pallas_call(functools.partial(kernel, rows, cols), out_shape=out, in_s...  20.4 us
    squeeze x1, local copies, waits for them, and re-layouts, local(): return (both[0], both[1])  0.66 us

profile of v7, /device:TPU:193, one launch (start us, length us, event | category | flops | bytes accessed | tf_op | source)
XLA Modules:
  0.0 21.7 jit_solution(9418600746107392837)
XLA Ops:
  0.6 20.4 %fracture.1 = f32[2,128,128]{2,1,0:T(8,128)S(1)} custom-call(f32[128,128]{1,0:T(8,128)} %opening_ref.1, f32[128,128]{1,0:T(8,128)} %pressure_ref.1, f32[128,128]{1,0:T(8,128)} %injection_ref.1, s32[1,64]{1,0:T(1,128)} %flags_ref.1, f32[256,256]{1,0:T(8,128)} %self_ref.1, s32[4,64]{1,0:T(4,128)} %bitcast.17, s32[4,64]{1,0:T(4,128)} %bitcast.18, ...), custom_call_target="tpu_custom_call" | custom-call | tf_op jit(solution)/shard_map/fracture/pallas_call | solution.py:343
  21.0 0.7 %slice_bitcast_fusion = (f32[128,128]{1,0:T(8,128)}, f32[128,128]{1,0:T(8,128)}) fusion(f32[2,128,128]{2,1,0:T(8,128)S(1)} %fracture.1), kind=kLoop, calls=%fused_computation | loop fusion | bytes 262144 | tf_op jit(solution)/shard_map/squeeze | solution.py:383
